TPU v7x, 32 devices: a whole 2x2x4 slice. The times are simulated.
32 devices in a mesh: rep: 4 (over z), sp: 8 (over y, x, core).
Axes of the slice: x: 2, y: 2, z: 4, core: 2. Of those that a mesh axis runs over, the one named last changes fastest.
Arguments:
- inputs: bfloat16 [4, 8, 16, 4096], P('rep', 'sp'), may hold values from -6 to 6
- preact: bfloat16 [4, 8, 16, 4096], P('rep', 'sp'), may hold values from -6 to 6
- grad_out: bfloat16 [4, 8, 16, 4096], P('rep', 'sp'), may hold values from -20 to 20
- weight: bfloat16 [3, 3, 3, 64, 64], replicated, may hold values from -0.15625 to 0.15625
Outputs:
- input_grad: bfloat16 [4, 8, 16, 4096], P('rep', 'sp')
- weight_grad: float32 [3, 3, 3, 64, 64], replicated
- bias_grad: float32 [64], replicated
All inputs are finite; a program needn't handle non-finite values.
Results may differ from a plain program's by a relative error of at most 0.001.
Values may be sent and summed in bfloat16 or wider, within the bound.
A program may use at most 64 MiB of HBM per device.

v0:
```python
import jax
import jax.numpy as jnp
from jax import lax
from jax.sharding import PartitionSpec as P


def with_halo(cells, sides, width):
    for axis, dim in sides:
        count = lax.axis_size(axis)
        ends = count - 1
        head = lax.slice_in_dim(cells, 0, width, axis=dim)
        tail = lax.slice_in_dim(cells, cells.shape[dim] - width, cells.shape[dim], axis=dim)
        cells = jnp.concatenate(
            [
                lax.ppermute(tail, axis, [(i, (i + 1) % count) for i in range(ends)]),
                cells,
                lax.ppermute(head, axis, [((i + 1) % count, i) for i in range(ends)]),
            ],
            axis=dim,
        )
    return cells


def unfold(volume, channels):
    samples, planes, height, packed = volume.shape
    cells = packed // channels
    shaped = volume.reshape(samples, planes, height, cells, channels)
    padded = jnp.pad(shaped, ((0, 0), (0, 0), (1, 1), (1, 1), (0, 0)))
    pieces = []
    for tap_h in range(3):
        for tap_w in range(3):
            pieces.append(padded[:, :, tap_h : tap_h + height, tap_w : tap_w + cells, :])
    stacked = jnp.concatenate(pieces, axis=4)
    return stacked.reshape(-1, 9 * channels)


def on_device(inputs, preact, grad_out, weight):
    channels = weight.shape[3]
    planes = inputs.shape[1]
    grad_masked = jnp.where(preact > 0, grad_out, jnp.zeros_like(grad_out))
    grad_padded = with_halo(grad_masked, (("sp", 1),), 1)
    flipped = jnp.transpose(weight[::-1, ::-1, ::-1], (0, 1, 2, 4, 3))
    grad_flat = grad_masked.reshape(-1, channels)
    input_padded = with_halo(inputs, (("sp", 1),), 1)
    totals = jnp.zeros((grad_flat.shape[0], channels), jnp.float32)
    kernel_rows = []
    for depth_tap in range(3):
        grad_cols = unfold(grad_padded[:, depth_tap : depth_tap + planes], channels)
        totals = totals + jnp.dot(
            grad_cols,
            flipped[depth_tap].reshape(9 * channels, channels),
            preferred_element_type=jnp.float32,
        )
        input_cols = unfold(input_padded[:, depth_tap : depth_tap + planes], channels)
        part = lax.dot_general(
            input_cols, grad_flat, (((0,), (0,)), ((), ())), preferred_element_type=jnp.float32
        )
        kernel_rows.append(part.reshape(3, 3, channels, channels))
    kernel_local = jnp.stack(kernel_rows, axis=0)
    bias_local = jnp.sum(grad_flat.astype(jnp.float32), axis=0)
    kernel_sum, bias_sum = lax.psum((kernel_local, bias_local), ("rep", "sp"))
    height = inputs.shape[2]
    cells = inputs.shape[3] // channels
    count = inputs.shape[0] * lax.axis_size("rep") * planes * lax.axis_size("sp") * height * cells
    scale = 1.0 / float(count) ** 0.5
    input_grad = totals.reshape(inputs.shape).astype(jnp.bfloat16)
    return (input_grad, kernel_sum * scale, bias_sum * scale)


def solution(mesh):
    return jax.shard_map(
        on_device,
        mesh=mesh,
        in_specs=(
            P("rep", "sp", None, None),
            P("rep", "sp", None, None),
            P("rep", "sp", None, None),
            P(),
        ),
        out_specs=(P("rep", "sp", None, None), P(), P()),
        check_vma=False,
    )
```

profile of v0, /device:TPU:0, one launch (start us, length us, event | category | flops | bytes accessed | tf_op | source)
XLA Modules:
  0.0 237.8 jit_solution(5133463988657181988)
XLA Ops:
  7.2 1.0 compare_select_fusion
  8.3 1.3 collective-permute-start.1
  9.6 3.7 %collective-permute-start = (bf16[1,1,16,4096]{3,2,1,0:T(8,128)(2,1)S(1)}, bf16[1,1,16,4096]{3,2,1,0:T(8,128)(2,1)}, u32[]{:S(2)}, u32[]{:S(2)}) collective-permute-start(bf16[1,1,16,4096]{3,2,1,0:T(8,128)(2,1)S(1)} %compare_select_fusion), channel_id=1, source_target_pairs={{0,1},{1,2},{2,3},{3,4},{4,5},{5,6},{6,7},{8,9},{9,10},{10,11},{11... | collective-permute-start | bytes 393224 | tf_op jit(solution)/shard_map/ppermute | solution.py:15
  13.3 1.3 collective-permute-start.3
  14.6 5.1 %collective-permute-start.2 = (bf16[1,1,16,4096]{3,2,1,0:T(8,128)(2,1)}, bf16[1,1,16,4096]{3,2,1,0:T(8,128)(2,1)}, u32[]{:S(2)}, u32[]{:S(2)}) collective-permute-start(bf16[1,1,16,4096]{3,2,1,0:T(8,128)(2,1)} %param.4), channel_id=1, source_target_pairs={{0,1},{1,2},{2,3},{3,4},{4,5},{5,6},{6,7},{8,9},{9,10},{10,11},{11... | collective-permute-start | bytes 393224 | tf_op jit(solution)/shard_map/ppermute | solution.py:15
  20.2 1.2 reshape.128
  23.2 1.5 pad_slice_fusion.32
  25.6 1.4 pad_slice_fusion.8
  27.1 2.6 %concatenate.181 = bf16[1024,576]{1,0:T(8,128)(2,1)S(1)} concatenate(bf16[1024,64]{1,0:T(8,128)(2,1)} %bitcast.160, bf16[1024,64]{1,0:T(8,128)(2,1)S(1)} %bitcast.154, bf16[1024,64]{1,0:T(8,128)(2,1)S(1)} %bitcast.155, bf16[1024,64]{1,0:T(8,128)(2,1)S(1)} %bitcast.156, bf16[1024,64]{1,0:T(8,128)(2,1)} %concatenate.176, bf16[1024,64]{1,0:T(8,128)(2,1)} %bitcast.157, ...), dimensions={1} | concatenate | bytes 2359296 | tf_op jit(solution)/shard_map/concatenate | solution.py:33
  30.4 41.9 %psum.15 = f32[64]{0:T(128)S(1)} all-reduce(f32[64]{0:T(128)S(1)} %convert_reduce_fusion), channel_id=1, replica_groups=mesh['rep'=4,'sp'=8] {'rep','sp'}, use_global_device_ids=true, to_apply=%region_2.3 | all-reduce | flops 64 | bytes 512 | tf_op jit(solution)/shard_map/psum | solution.py:61
  72.9 2.6 %concatenate.151 = bf16[1024,576]{1,0:T(8,128)(2,1)S(1)} concatenate(bf16[1024,64]{1,0:T(8,128)(2,1)} %bitcast.136, bf16[1024,64]{1,0:T(8,128)(2,1)S(1)} %bitcast.130, bf16[1024,64]{1,0:T(8,128)(2,1)} %bitcast.131, bf16[1024,64]{1,0:T(8,128)(2,1)} %bitcast.132, bf16[1024,64]{1,0:T(8,128)(2,1)S(1)} %concatenate.146, bf16[1024,64]{1,0:T(8,128)(2,1)} %bitcast.133, ...), dimensions={1} | concatenate | bytes 2359296 | tf_op jit(solution)/shard_map/concatenate | solution.py:33
  75.5 1.3 fusion.6
  77.2 1.2 reshape.130
  78.4 1.3 pad_slice_fusion
  79.7 1.9 concatenate.186
  81.6 2.5 %concatenate.191 = bf16[1024,576]{1,0:T(8,128)(2,1)S(1)} concatenate(bf16[1024,64]{1,0:T(8,128)(2,1)} %bitcast.144, bf16[1024,64]{1,0:T(8,128)(2,1)S(1)} %bitcast.138, bf16[1024,64]{1,0:T(8,128)(2,1)S(1)} %bitcast.139, bf16[1024,64]{1,0:T(8,128)(2,1)S(1)} %bitcast.140, bf16[1024,64]{1,0:T(8,128)(2,1)} %concatenate.186, bf16[1024,64]{1,0:T(8,128)(2,1)S(1)} %bitcast.141, ...), dimensions={1} | concatenate | bytes 2359296 | tf_op jit(solution)/shard_map/concatenate | solution.py:33
  85.3 1.2 reshape.125
  86.4 1.6 pad_slice_fusion.24
  88.1 1.2 reshape.123
  89.3 1.6 pad_slice_fusion.40
  90.9 1.2 reshape.126
  92.1 1.3 pad_slice_fusion.16
  93.4 1.9 concatenate.166
  95.3 2.5 %concatenate.171 = bf16[1024,576]{1,0:T(8,128)(2,1)S(1)} concatenate(bf16[1024,64]{1,0:T(8,128)(2,1)} %bitcast.152, bf16[1024,64]{1,0:T(8,128)(2,1)S(1)} %bitcast.146, bf16[1024,64]{1,0:T(8,128)(2,1)S(1)} %bitcast.147, bf16[1024,64]{1,0:T(8,128)(2,1)S(1)} %bitcast.148, bf16[1024,64]{1,0:T(8,128)(2,1)} %concatenate.166, bf16[1024,64]{1,0:T(8,128)(2,1)S(1)} %bitcast.149, ...), dimensions={1} | concatenate | bytes 2359296 | tf_op jit(solution)/shard_map/concatenate | solution.py:33
  100.0 2.0 concatenate.156
  102.0 2.4 %concatenate.161 = bf16[1024,576]{1,0:T(8,128)(2,1)S(1)} concatenate(bf16[1024,64]{1,0:T(8,128)(2,1)S(1)} %bitcast.128, bf16[1024,64]{1,0:T(8,128)(2,1)S(1)} %bitcast.122, bf16[1024,64]{1,0:T(8,128)(2,1)S(1)} %bitcast.123, bf16[1024,64]{1,0:T(8,128)(2,1)S(1)} %bitcast.124, bf16[1024,64]{1,0:T(8,128)(2,1)} %concatenate.156, bf16[1024,64]{1,0:T(8,128)(2,1)S(1)} %bitcast.125, ...), dimensions={1} | concatenate | bytes 2359296 | tf_op jit(solution)/shard_map/concatenate | solution.py:33
  104.5 1.2 fusion.7
  105.7 1.9 concatenate.136
  107.7 2.4 %concatenate.141 = bf16[1024,576]{1,0:T(8,128)(2,1)S(1)} concatenate(bf16[1024,64]{1,0:T(8,128)(2,1)S(1)} %bitcast.120, bf16[1024,64]{1,0:T(8,128)(2,1)S(1)} %bitcast.114, bf16[1024,64]{1,0:T(8,128)(2,1)S(1)} %bitcast.115, bf16[1024,64]{1,0:T(8,128)(2,1)S(1)} %bitcast.116, bf16[1024,64]{1,0:T(8,128)(2,1)} %concatenate.136, bf16[1024,64]{1,0:T(8,128)(2,1)S(1)} %bitcast.117, ...), dimensions={1} | concatenate | bytes 2359296 | tf_op jit(solution)/shard_map/concatenate | solution.py:33
  110.1 1.6 fusion.1
  112.8 116.0 %all-reduce.8.cloned.1.call-done = f32[3,3,3,64,64]{4,3,2,1,0:T(8,128)} async-done(((f32[3,3,3,64,64]{4,3,2,1,0:T(8,128)}), f32[3,3,3,64,64]{4,3,2,1,0:T(8,128)}) %all-reduce.8.cloned.1.call-update) | async-done | bytes 442384 | tf_op jit(solution)/shard_map/psum | solution.py:61
  228.8 2.2 broadcast_multiply_fusion
  (65 shorter events, 9.4 us)
Async XLA Ops:
  7.2 14.2 %copy-start.18 = (bf16[1,1,16,4096]{3,2,1,0:T(8,128)(2,1)S(1)}, bf16[1,1,16,4096]{3,2,1,0:T(8,128)(2,1)}, u32[]{:S(2)}) copy-start(bf16[1,1,16,4096]{3,2,1,0:T(8,128)(2,1)} %param.4) | copy-start | bytes 393220
  7.2 15.2 %copy-start.19 = (bf16[3,3,3,64,64]{4,3,2,1,0:T(8,128)(2,1)S(1)}, bf16[3,3,3,64,64]{4,3,2,1,0:T(8,128)(2,1)}, u32[]{:S(2)}) copy-start(bf16[3,3,3,64,64]{4,3,2,1,0:T(8,128)(2,1)} %param.7) | copy-start | bytes 663556
  7.2 221.6 %all-reduce.8.cloned.1.call-start = ((), (), s32[]{:S(2)}) async-start(), calls=%async_computation | async-start | bytes 1769472 | tf_op jit(solution)/shard_map/psum | solution.py:61
  8.3 77.0 %collective-permute-start.1 = (bf16[1,1,16,4096]{3,2,1,0:T(8,128)(2,1)S(1)}, bf16[1,1,16,4096]{3,2,1,0:T(8,128)(2,1)}, u32[]{:S(2)}, u32[]{:S(2)}) collective-permute-start(bf16[1,1,16,4096]{3,2,1,0:T(8,128)(2,1)S(1)} %compare_select_fusion), channel_id=1, source_target_pairs={{1,0},{2,1},{3,2},{4,3},{5,4},{6,5},{7,6},{9,8},{10,9},{11,10},{12... | collective-permute-start | bytes 393224 | tf_op jit(solution)/shard_map/ppermute | solution.py:17
  9.6 78.5 %collective-permute-start = (bf16[1,1,16,4096]{3,2,1,0:T(8,128)(2,1)S(1)}, bf16[1,1,16,4096]{3,2,1,0:T(8,128)(2,1)}, u32[]{:S(2)}, u32[]{:S(2)}) collective-permute-start(bf16[1,1,16,4096]{3,2,1,0:T(8,128)(2,1)S(1)} %compare_select_fusion), channel_id=1, source_target_pairs={{0,1},{1,2},{2,3},{3,4},{4,5},{5,6},{6,7},{8,9},{9,10},{10,11},{11... | collective-permute-start | bytes 393224 | tf_op jit(solution)/shard_map/ppermute | solution.py:15
  13.3 63.9 %collective-permute-start.3 = (bf16[1,1,16,4096]{3,2,1,0:T(8,128)(2,1)}, bf16[1,1,16,4096]{3,2,1,0:T(8,128)(2,1)}, u32[]{:S(2)}, u32[]{:S(2)}) collective-permute-start(bf16[1,1,16,4096]{3,2,1,0:T(8,128)(2,1)} %param.4), channel_id=1, source_target_pairs={{1,0},{2,1},{3,2},{4,3},{5,4},{6,5},{7,6},{9,8},{10,9},{11,10},{12... | collective-permute-start | bytes 393224 | tf_op jit(solution)/shard_map/ppermute | solution.py:17
  14.6 76.4 %collective-permute-start.2 = (bf16[1,1,16,4096]{3,2,1,0:T(8,128)(2,1)}, bf16[1,1,16,4096]{3,2,1,0:T(8,128)(2,1)}, u32[]{:S(2)}, u32[]{:S(2)}) collective-permute-start(bf16[1,1,16,4096]{3,2,1,0:T(8,128)(2,1)} %param.4), channel_id=1, source_target_pairs={{0,1},{1,2},{2,3},{3,4},{4,5},{5,6},{6,7},{8,9},{9,10},{10,11},{11... | collective-permute-start | bytes 393224 | tf_op jit(solution)/shard_map/ppermute | solution.py:15
  98.9 3.0 %copy-start.8 = (bf16[1,1,16,64,64]{4,3,2,1,0:T(8,128)(2,1)S(1)}, bf16[1,1,16,64,64]{4,3,2,1,0:T(8,128)(2,1)}, u32[]{:S(2)}) copy-start(bf16[1,1,16,64,64]{4,3,2,1,0:T(8,128)(2,1)} %get-tuple-element.46) | copy-start | bytes 393220
  98.9 3.0 %copy-start.9 = (bf16[1,1,16,64,64]{4,3,2,1,0:T(8,128)(2,1)S(1)}, bf16[1,1,16,64,64]{4,3,2,1,0:T(8,128)(2,1)}, u32[]{:S(2)}) copy-start(bf16[1,1,16,64,64]{4,3,2,1,0:T(8,128)(2,1)} %get-tuple-element.47) | copy-start | bytes 393220
  98.9 3.0 %copy-start.10 = (bf16[1,1,16,64,64]{4,3,2,1,0:T(8,128)(2,1)S(1)}, bf16[1,1,16,64,64]{4,3,2,1,0:T(8,128)(2,1)}, u32[]{:S(2)}) copy-start(bf16[1,1,16,64,64]{4,3,2,1,0:T(8,128)(2,1)} %get-tuple-element.48) | copy-start | bytes 393220
  99.0 3.0 %copy-start.11 = (bf16[1,1,16,64,64]{4,3,2,1,0:T(8,128)(2,1)S(1)}, bf16[1,1,16,64,64]{4,3,2,1,0:T(8,128)(2,1)}, u32[]{:S(2)}) copy-start(bf16[1,1,16,64,64]{4,3,2,1,0:T(8,128)(2,1)} %get-tuple-element.49) | copy-start | bytes 393220
  99.0 3.0 %copy-start.12 = (bf16[1,1,16,64,64]{4,3,2,1,0:T(8,128)(2,1)S(1)}, bf16[1,1,16,64,64]{4,3,2,1,0:T(8,128)(2,1)}, u32[]{:S(2)}) copy-start(bf16[1,1,16,64,64]{4,3,2,1,0:T(8,128)(2,1)} %get-tuple-element.50) | copy-start | bytes 393220
  99.0 3.0 %copy-start.13 = (bf16[1,1,16,64,64]{4,3,2,1,0:T(8,128)(2,1)S(1)}, bf16[1,1,16,64,64]{4,3,2,1,0:T(8,128)(2,1)}, u32[]{:S(2)}) copy-start(bf16[1,1,16,64,64]{4,3,2,1,0:T(8,128)(2,1)} %get-tuple-element.51) | copy-start | bytes 393220
  100.0 2.0 copy-start.14
  100.0 2.0 copy-start.15
  102.0 2.5 %copy-start.17 = (bf16[1,3,3,64,64]{4,3,2,1,0:T(8,128)(2,1)S(1)}, bf16[1,3,3,64,64]{4,3,2,1,0:T(8,128)(2,1)}, u32[]{:S(2)}) copy-start(bf16[1,3,3,64,64]{4,3,2,1,0:T(8,128)(2,1)} %copy.39) | copy-start | bytes 221188
  104.4 3.2 %copy-start = (bf16[1,1,16,64,64]{4,3,2,1,0:T(8,128)(2,1)S(1)}, bf16[1,1,16,64,64]{4,3,2,1,0:T(8,128)(2,1)}, u32[]{:S(2)}) copy-start(bf16[1,1,16,64,64]{4,3,2,1,0:T(8,128)(2,1)} %get-tuple-element.30) | copy-start | bytes 393220
  104.4 3.2 %copy-start.1 = (bf16[1,1,16,64,64]{4,3,2,1,0:T(8,128)(2,1)S(1)}, bf16[1,1,16,64,64]{4,3,2,1,0:T(8,128)(2,1)}, u32[]{:S(2)}) copy-start(bf16[1,1,16,64,64]{4,3,2,1,0:T(8,128)(2,1)} %get-tuple-element.31) | copy-start | bytes 393220
  104.4 3.2 %copy-start.2 = (bf16[1,1,16,64,64]{4,3,2,1,0:T(8,128)(2,1)S(1)}, bf16[1,1,16,64,64]{4,3,2,1,0:T(8,128)(2,1)}, u32[]{:S(2)}) copy-start(bf16[1,1,16,64,64]{4,3,2,1,0:T(8,128)(2,1)} %get-tuple-element.32) | copy-start | bytes 393220
  104.4 3.2 %copy-start.3 = (bf16[1,1,16,64,64]{4,3,2,1,0:T(8,128)(2,1)S(1)}, bf16[1,1,16,64,64]{4,3,2,1,0:T(8,128)(2,1)}, u32[]{:S(2)}) copy-start(bf16[1,1,16,64,64]{4,3,2,1,0:T(8,128)(2,1)} %get-tuple-element.33) | copy-start | bytes 393220
  104.4 3.2 %copy-start.4 = (bf16[1,1,16,64,64]{4,3,2,1,0:T(8,128)(2,1)S(1)}, bf16[1,1,16,64,64]{4,3,2,1,0:T(8,128)(2,1)}, u32[]{:S(2)}) copy-start(bf16[1,1,16,64,64]{4,3,2,1,0:T(8,128)(2,1)} %get-tuple-element.34) | copy-start | bytes 393220
  104.5 3.2 %copy-start.5 = (bf16[1,1,16,64,64]{4,3,2,1,0:T(8,128)(2,1)S(1)}, bf16[1,1,16,64,64]{4,3,2,1,0:T(8,128)(2,1)}, u32[]{:S(2)}) copy-start(bf16[1,1,16,64,64]{4,3,2,1,0:T(8,128)(2,1)} %get-tuple-element.35) | copy-start | bytes 393220
  104.5 3.2 %copy-start.6 = (bf16[1,1,16,64,64]{4,3,2,1,0:T(8,128)(2,1)S(1)}, bf16[1,1,16,64,64]{4,3,2,1,0:T(8,128)(2,1)}, u32[]{:S(2)}) copy-start(bf16[1,1,16,64,64]{4,3,2,1,0:T(8,128)(2,1)} %get-tuple-element.36) | copy-start | bytes 393220
  104.5 3.2 %copy-start.7 = (bf16[1,1,16,64,64]{4,3,2,1,0:T(8,128)(2,1)S(1)}, bf16[1,1,16,64,64]{4,3,2,1,0:T(8,128)(2,1)}, u32[]{:S(2)}) copy-start(bf16[1,1,16,64,64]{4,3,2,1,0:T(8,128)(2,1)} %get-tuple-element.37) | copy-start | bytes 393220
  107.7 2.4 %copy-start.16 = (bf16[1,3,3,64,64]{4,3,2,1,0:T(8,128)(2,1)S(1)}, bf16[1,3,3,64,64]{4,3,2,1,0:T(8,128)(2,1)}, u32[]{:S(2)}) copy-start(bf16[1,3,3,64,64]{4,3,2,1,0:T(8,128)(2,1)} %copy.37) | copy-start | bytes 221188
Sparse Core Ops, SparseCore 0:
  100.1 128.5 all-reduce.7
where the time goes:
time: 239 us; the launch traced here: 238 us
  waiting for transfers between devices  116 us (49%)
  local copies, waits for them, and re-layouts  43.7 us (18%)
  blocking collectives  41.9 us (18%)
  between operations  14.5 us (6%)
  starting transfers between devices  11.4 us (5%)
  matrix products  5.47 us (2%)
  other arithmetic  4.88 us (2%)
    psum x1, waiting for transfers between devices, on_device(): kernel_sum, bias_sum = lax.psum((kernel_local, bias_local), ('rep', 'sp'))  116 us
    psum x1, blocking collectives, on_device(): kernel_sum, bias_sum = lax.psum((kernel_local, bias_local), ('rep', 'sp'))  41.9 us
    concatenate x12, local copies, waits for them, and re-layouts, unfold(): stacked = jnp.concatenate(pieces, axis=4)  23.9 us
    slice x6, local copies, waits for them, and re-layouts, unfold(): pieces.append(padded[:, :, tap_h:tap_h + height, tap_w:tap_w + cells, :])  8.85 us
    ppermute x2, starting transfers between devices, with_halo(): lax.ppermute(tail, axis, [(i, (i + 1) % count) for i in range(ends)])  8.81 us
    reshape x6, local copies, waits for them, and re-layouts, unfold(): shaped = volume.reshape(samples, planes, height, cells, channels)  6.14 us
  transfers between devices with their start and end apart: 5, of which 1 were waited for; matrix products, arithmetic and copies ran while one was open for 18% of the time, Pallas kernels for 0%

commit v1 on v0

v1 whole, which is shorter than its diff:
```python
import functools

import jax
import jax.numpy as jnp
from jax import lax
from jax.experimental import pallas as pl
from jax.experimental.pallas import tpu as pltpu
from jax.sharding import PartitionSpec as P

MESH = pl.DeviceIdType.MESH
F32 = jnp.float32
BF16 = jnp.bfloat16


def round_up(value, step):
    return -(-value // step) * step


def to_rows(plane, lanes):
    count = plane.shape[1] // lanes
    return jnp.concatenate([plane[:, j * lanes : (j + 1) * lanes] for j in range(count)], axis=0)


def shift_rows(rows, offset, height):
    place = lax.broadcasted_iota(jnp.int32, rows.shape, 0) % height
    moved = pltpu.roll(rows, (-offset) % rows.shape[0], 0)
    inside = (place + offset >= 0) & (place + offset < height)
    return jnp.where(inside, moved, jnp.zeros_like(moved))


def kernel(
    n_rep, n_sp, scale,
    x_ref, z_ref, dy_ref, w_ref,
    dx_ref, wg_ref, bg_ref,
    gbuf, halo, xt, wn, gc, acc, pair_in, mid, xy_in, z_in, z_own, z_all, full,
    halo_send, halo_recv, pair_send, pair_recv, xy_send, xy_recv, z_send, z_recv,
    zg_send, zg_recv, xg_send, xg_recv, pg_send, pg_recv,
):
    height = x_ref.shape[2]
    ch = w_ref.shape[3]
    lanes = 2 * ch
    rows = height * x_ref.shape[3] // lanes
    n_chip = n_sp // 2
    part = xy_in.shape[1]
    half = n_chip * part
    zpart = z_in.shape[1]

    rep, sp = lax.axis_index("rep"), lax.axis_index("sp")
    core, chip = sp % 2, sp // 2
    pair = chip * 2 + 1 - core
    far = sp + 2 * core - 1
    has_far = (far >= 0) & (far < n_sp)

    def chip_at(step):
        return lax.rem(chip + step, n_chip)

    def rep_at(step):
        return lax.rem(rep + step, n_rep)

    barrier = pltpu.get_barrier_semaphore()

    def greet(**where):
        pl.semaphore_signal(barrier, inc=1, device_id=where, device_id_type=MESH)

    greet(sp=pair)
    for t in range(1, n_chip):
        greet(sp=chip_at(t) * 2 + core)
    for t in range(1, n_rep):
        greet(rep=rep_at(t))

    @pl.when(has_far)
    def _():
        greet(sp=far)

    keep = z_ref[0, 0].astype(F32) > 0
    g_plane = jnp.where(keep, dy_ref[0, 0].astype(F32), 0.0)
    gbuf[...] = g_plane.astype(BF16)

    pl.semaphore_wait(barrier, n_chip + n_rep - 1 + jnp.where(has_far, 1, 0))

    def copy(src, dst, send, recv, **where):
        return pltpu.make_async_remote_copy(
            src_ref=src, dst_ref=dst, send_sem=send, recv_sem=recv,
            device_id=where, device_id_type=MESH,
        )

    near_copy = copy(gbuf, halo.at[core], halo_send.at[0], halo_recv.at[0], sp=pair)
    far_copy = copy(gbuf, halo.at[1 - core], halo_send.at[1], halo_recv.at[1], sp=far)

    @pl.when(has_far)
    def _():
        far_copy.start()

    near_copy.start()

    @pl.when(jnp.logical_not(has_far))
    def _():
        halo[core] = jnp.zeros_like(gbuf)

    x_rows = to_rows(x_ref[0, 0].astype(F32), lanes)
    for k, oh in enumerate((-1, 0, 1)):
        xt[k * lanes : (k + 1) * lanes, :] = shift_rows(x_rows, oh, height).astype(BF16).T

    zero_tap = jnp.zeros((ch, ch), BF16)
    for od in range(3):
        for oh in range(3):
            w_m, w_0, w_p = w_ref[od, oh, 0], w_ref[od, oh, 1], w_ref[od, oh, 2]
            r, c = oh * lanes, od * 2 * lanes
            grid = ((w_0, w_m, w_p, zero_tap), (w_p, w_0, zero_tap, w_m))
            for a in range(2):
                for b in range(4):
                    wn[r + a * ch : r + (a + 1) * ch, c + b * ch : c + (b + 1) * ch] = grid[a][b]

    left = lax.broadcasted_iota(jnp.int32, (rows, lanes), 1) < ch
    left_tile = lax.broadcasted_iota(jnp.int32, (ch, lanes), 1) < ch

    def spread(g_rows, od):
        turned = pltpu.roll(g_rows, ch, 1)
        gap = jnp.zeros((height, lanes), F32)
        before = jnp.concatenate([gap, turned[:-height]], axis=0)
        after = jnp.concatenate([turned[height:], gap], axis=0)
        c = od * 2 * lanes
        gc[:, c : c + lanes] = g_rows.astype(BF16)
        gc[:, c + lanes : c + 2 * lanes] = jnp.where(left, before, after).astype(BF16)

    middles = [None] * 9

    def taps(od):
        c = od * 2 * lanes
        prod = jnp.dot(xt[...], gc[:, c : c + 2 * lanes], preferred_element_type=F32)
        for oh in range(3):
            r = oh * lanes
            own0, own1 = prod[r : r + ch, :lanes], prod[r + ch : r + 2 * ch, :lanes]
            mix0, mix1 = prod[r : r + ch, lanes:], prod[r + ch : r + 2 * ch, lanes:]
            u = od * 3 + oh
            acc[u * ch : (u + 1) * ch, :] = jnp.where(left_tile, own1 + mix0, own0 + mix1)
            same = jnp.where(left_tile, own0, own1)
            middles[u] = same + pltpu.roll(same, ch, 1)

    g_rows = to_rows(g_plane, lanes)
    spread(g_rows, 1)
    taps(1)
    bias = jnp.sum(g_rows, axis=0, keepdims=True)
    bias = bias + pltpu.roll(bias, ch, 1)

    near_copy.wait_recv()

    @pl.when(has_far)
    def _():
        far_copy.wait_recv()

    spread(to_rows(halo[1].astype(F32), lanes), 0)
    spread(to_rows(halo[0].astype(F32), lanes), 2)
    taps(0)
    taps(2)
    others = middles + [jnp.broadcast_to(bias, (ch, lanes))]
    for m in range(5):
        u = 9 + m
        acc[u * ch : (u + 1) * ch, :] = jnp.where(left_tile, others[2 * m], others[2 * m + 1])
    if acc.shape[0] > 14 * ch:
        acc[14 * ch :, :] = jnp.zeros((acc.shape[0] - 14 * ch, lanes), F32)

    theirs = acc.at[pl.ds(pl.multiple_of((1 - core) * half, 8), half)]
    pair_copy = copy(theirs, pair_in, pair_send, pair_recv, sp=pair)
    pair_copy.start()

    step = 8 * height
    for s in range(0, rows, step):
        y = lax.dot_general(
            gc[s : s + step, :], wn[...], (((1,), (1,)), ((), ())), preferred_element_type=F32
        )
        total = y[:, lanes : 2 * lanes]
        total = total + shift_rows(y[:, :lanes], 1, height)
        total = total + shift_rows(y[:, 2 * lanes :], -1, height)
        total = total.astype(BF16)
        for j in range(step // height):
            c = (s // height + j) * lanes
            dx_ref[0, 0, :, c : c + lanes] = total[j * height : (j + 1) * height]

    pair_copy.wait_recv()
    mid[...] = acc[pl.ds(pl.multiple_of(core * half, 8), half), :] + pair_in[...]

    xy_copies = []
    for t in range(1, n_chip):
        to = chip_at(t)
        block = mid.at[pl.ds(pl.multiple_of(to * part, 8), part)]
        c = copy(block, xy_in.at[t - 1], xy_send.at[t - 1], xy_recv.at[t - 1], sp=to * 2 + core)
        c.start()
        xy_copies.append(c)
    own = mid[pl.ds(pl.multiple_of(chip * part, 8), part), :]
    for t in range(1, n_chip):
        xy_copies[t - 1].wait_recv()
        own = own + xy_in[t - 1]
    z_own[...] = own

    def z_start(k):
        return pl.multiple_of(jnp.minimum(k * zpart, part - zpart), 8)

    z_copies = []
    for t in range(1, n_rep):
        to = rep_at(t)
        block = z_own.at[pl.ds(z_start(to), zpart)]
        c = copy(block, z_in.at[rep], z_send.at[t - 1], z_recv.at[t - 1], rep=to)
        c.start()
        z_copies.append(c)
    z_in[rep] = z_own[pl.ds(z_start(rep), zpart), :]
    for c in z_copies:
        c.wait_recv()
    z_all[rep] = functools.reduce(lambda p, q: p + q, [z_in[k] for k in range(n_rep)]) * scale

    zg_copies = []
    for t in range(1, n_rep):
        c = copy(z_all.at[rep], z_all.at[rep], zg_send.at[t - 1], zg_recv.at[t - 1], rep=rep_at(t))
        c.start()
        zg_copies.append(c)
    for c in zg_copies:
        c.wait_recv()
    for k in range(n_rep):
        at = min(k * zpart, part - zpart)
        full[core, chip, at : at + zpart, :] = z_all[k]

    mine = full.at[core, chip]
    xg_copies = []
    for t in range(1, n_chip):
        c = copy(mine, mine, xg_send.at[t - 1], xg_recv.at[t - 1], sp=chip_at(t) * 2 + core)
        c.start()
        xg_copies.append(c)
    pg_copies = [copy(mine, mine, pg_send.at[0], pg_recv.at[0], sp=pair)]
    pg_copies[0].start()
    for t in range(1, n_chip):
        xg_copies[t - 1].wait_recv()
        came = full.at[core, lax.rem(chip + n_chip - t, n_chip)]
        c = copy(came, came, pg_send.at[t], pg_recv.at[t], sp=pair)
        c.start()
        pg_copies.append(c)
    for c in pg_copies:
        c.wait_recv()

    flat = full.reshape(2 * half, lanes)
    for od in range(3):
        for oh in range(3):
            u = od * 3 + oh
            tile = flat[u * ch : (u + 1) * ch, :]
            wg_ref[od, oh, 2] = tile[:, :ch]
            wg_ref[od, oh, 0] = tile[:, ch:]
            v = 9 + u // 2
            tile = flat[v * ch : (v + 1) * ch, :]
            wg_ref[od, oh, 1] = tile[:, :ch] if u % 2 == 0 else tile[:, ch:]
    bg_ref[...] = flat[13 * ch : 13 * ch + 1, :][:, ch:]

    near_copy.wait_send()

    @pl.when(has_far)
    def _():
        far_copy.wait_send()

    for c in [pair_copy] + xy_copies + z_copies + zg_copies + xg_copies + pg_copies:
        c.wait_send()


def on_device(n_rep, n_sp, inputs, preact, grad_out, weight):
    ch = weight.shape[3]
    height, packed = inputs.shape[2:]
    lanes = 2 * ch
    rows = height * packed // lanes
    n_chip = n_sp // 2
    count = inputs.shape[0] * n_rep * inputs.shape[1] * n_sp * rows * 2
    part = round_up(-(-14 * ch // (2 * n_chip)), 8)
    zpart = min(part, round_up(-(-part // n_rep), 8))
    half = n_chip * part
    dma = pltpu.SemaphoreType.DMA
    vmem = pl.BlockSpec(memory_space=pltpu.VMEM)
    input_grad, weight_grad, bias_grad = pl.pallas_call(
        functools.partial(kernel, n_rep, n_sp, 1.0 / float(count) ** 0.5),
        out_shape=(
            jax.ShapeDtypeStruct(inputs.shape, BF16),
            jax.ShapeDtypeStruct(weight.shape, F32),
            jax.ShapeDtypeStruct((1, ch), F32),
        ),
        in_specs=[vmem] * 4,
        out_specs=(vmem, vmem, vmem),
        scratch_shapes=[
            pltpu.VMEM((height, packed), BF16),
            pltpu.VMEM((2, height, packed), BF16),
            pltpu.VMEM((3 * lanes, rows), BF16),
            pltpu.VMEM((3 * lanes, 6 * lanes), BF16),
            pltpu.VMEM((rows, 6 * lanes), BF16),
            pltpu.VMEM((2 * half, lanes), F32),
            pltpu.VMEM((half, lanes), F32),
            pltpu.VMEM((half, lanes), F32),
            pltpu.VMEM((max(n_chip - 1, 1), part, lanes), F32),
            pltpu.VMEM((n_rep, zpart, lanes), F32),
            pltpu.VMEM((part, lanes), F32),
            pltpu.VMEM((n_rep, zpart, lanes), F32),
            pltpu.VMEM((2, n_chip, part, lanes), F32),
            dma((2,)), dma((2,)),
            dma, dma,
            dma((n_chip,)), dma((n_chip,)),
            dma((n_rep,)), dma((n_rep,)),
            dma((n_rep,)), dma((n_rep,)),
            dma((n_chip,)), dma((n_chip,)),
            dma((n_chip,)), dma((n_chip,)),
        ],
        compiler_params=pltpu.CompilerParams(
            collective_id=0, has_side_effects=True, vmem_limit_bytes=40 * 1024 * 1024
        ),
    )(inputs, preact, grad_out, weight)
    return input_grad, weight_grad, bias_grad.reshape(ch)


def solution(mesh):
    split = P("rep", "sp", None, None)
    return jax.shard_map(
        functools.partial(on_device, mesh.shape["rep"], mesh.shape["sp"]),
        mesh=mesh,
        in_specs=(split, split, split, P()),
        out_specs=(split, P(), P()),
        check_vma=False,
    )
```

time: 239 us -> 35.5 us (0.15)
  waiting for transfers between devices: 116 us -> 0 us
  blocking collectives: 41.9 us -> 0 us
  local copies, waits for them, and re-layouts: 43.7 us -> 5.8 us
  Pallas kernels: 0 us -> 28.8 us
  between operations: 14.5 us -> 0.65 us
  starting transfers between devices: 11.4 us -> 0 us
  matrix products: 5.47 us -> 0 us
  other arithmetic: 4.88 us -> 0 us
    psum x1 -> x0, waiting for transfers between devices: 116 us -> none  [on_device(): kernel_sum, bias_sum = lax.psum((kernel_local, bias_local), ('rep', 'sp'))]
    psum x1 -> x0, blocking collectives: 41.9 us -> none  [on_device(): kernel_sum, bias_sum = lax.psum((kernel_local, bias_local), ('rep', 'sp'))]
    pallas_call x0 -> x1, Pallas kernels: none -> 28.8 us  [on_device(): pl.pallas_call(functools.partial(kernel, n_rep, n_sp, 1.0 / float(count)...]
    concatenate x12 -> x0, local copies, waits for them, and re-layouts: 23.9 us -> none  [unfold(): stacked = jnp.concatenate(pieces, axis=4)]
    ppermute x4 -> x0, starting transfers between devices: 11.4 us -> none  [the longest x2 8.81 us: with_halo(): lax.ppermute(tail, axis, [(i, (i + 1) % count) for i in range(ends)])]
    slice x10 -> x0, local copies, waits for them, and re-layouts: 10.6 us -> none  [the longest x6 8.85 us: unfold(): pieces.append(padded[:, :, tap_h:tap_h + height, tap_w:tap_w + cells, :])]
    reshape x6 -> x0, local copies, waits for them, and re-layouts: 6.14 us -> none  [unfold(): shaped = volume.reshape(samples, planes, height, cells, channels)]
    unnamed x40 -> x11, local copies, waits for them, and re-layouts: 0.09 us -> 5.8 us
  transfers between devices with their start and end apart: 5 -> 0, of which waited for: 1 -> 0; matrix products, arithmetic and copies ran while one was open for 18% -> 0% of each run, Pallas kernels for 0% -> 0%
where the time goes in v1:
time: 35.5 us; the launch traced here: 35.2 us
  Pallas kernels  28.8 us (81%)
  local copies, waits for them, and re-layouts  5.8 us (16%)
  between operations  0.65 us (2%)
    pallas_call x1, Pallas kernels, on_device(): pl.pallas_call(functools.partial(kernel, n_rep, n_sp, 1.0 / float(count)...  28.8 us
    unnamed x11, local copies, waits for them, and re-layouts  5.8 us

profile of v1, /device:TPU:0, one launch (start us, length us, event | category | flops | bytes accessed | tf_op | source)
XLA Modules:
  0.0 35.2 jit_solution(14002412502820146245)
XLA Ops:
  0.6 0.0 copy-start
  0.6 1.0 %copy-done = bf16[3,3,3,64,64]{4,3,2,1,0:T(8,128)(2,1)S(1)} copy-done((bf16[3,3,3,64,64]{4,3,2,1,0:T(8,128)(2,1)S(1)}, bf16[3,3,3,64,64]{4,3,2,1,0:T(8,128)(2,1)}, u32[]{:S(2)}) %copy-start) | copy-done | bytes 221208
  1.6 0.0 copy-start.1
  1.6 0.9 %copy-done.1 = bf16[1,1,16,4096]{3,2,1,0:T(8,128)(2,1)S(1)} copy-done((bf16[1,1,16,4096]{3,2,1,0:T(8,128)(2,1)S(1)}, bf16[1,1,16,4096]{3,2,1,0:T(8,128)(2,1)}, u32[]{:S(2)}) %copy-start.1) | copy-done | bytes 131096
  2.5 0.0 copy-start.2
  2.6 0.9 %copy-done.2 = bf16[1,1,16,4096]{3,2,1,0:T(8,128)(2,1)S(1)} copy-done((bf16[1,1,16,4096]{3,2,1,0:T(8,128)(2,1)S(1)}, bf16[1,1,16,4096]{3,2,1,0:T(8,128)(2,1)}, u32[]{:S(2)}) %copy-start.2) | copy-done | bytes 131096
  3.5 0.0 copy-start.3
  3.5 0.9 %copy-done.3 = bf16[1,1,16,4096]{3,2,1,0:T(8,128)(2,1)S(1)} copy-done((bf16[1,1,16,4096]{3,2,1,0:T(8,128)(2,1)S(1)}, bf16[1,1,16,4096]{3,2,1,0:T(8,128)(2,1)}, u32[]{:S(2)}) %copy-start.3) | copy-done | bytes 131096
  4.4 28.8 %shard_map.67 = (bf16[1,1,16,4096]{3,2,1,0:T(8,128)(2,1)S(1)}, f32[3,3,3,64,64]{4,3,2,1,0:T(8,128)S(1)}, f32[1,64]{1,0:T(1,128)S(1)}) custom-call(bf16[1,1,16,4096]{3,2,1,0:T(8,128)(2,1)S(1)} %copy-done.1, bf16[1,1,16,4096]{3,2,1,0:T(8,128)(2,1)S(1)} %copy-done.2, bf16[1,1,16,4096]{3,2,1,0:T(8,128)(2,1)S(1)} %copy-done.3, bf16[3,3,3,64,64]{4,3,2,1,0:T(8,128)(2,1)S(1)} %copy-done), custom_call_target="tpu_custom_call" | custom-call | tf_op jit(solution)/shard_map/pallas_call | solution.py:273
  33.1 0.7 %copy.10 = bf16[1,1,16,4096]{3,2,1,0:T(8,128)(2,1)} copy(bf16[1,1,16,4096]{3,2,1,0:T(8,128)(2,1)S(1)} %get-tuple-element.12) | data formatting | bytes 262144
  33.8 0.9 %copy.11 = f32[3,3,3,64,64]{4,3,2,1,0:T(8,128)} copy(f32[3,3,3,64,64]{4,3,2,1,0:T(8,128)S(1)} %get-tuple-element.13) | data formatting | bytes 884736
  34.7 0.5 %copy.12 = f32[64]{0:T(128)} copy(f32[64]{0:T(128)S(1)} %bitcast.1) | data formatting | bytes 512
Async XLA Ops:
  0.6 1.0 %copy-start = (bf16[3,3,3,64,64]{4,3,2,1,0:T(8,128)(2,1)S(1)}, bf16[3,3,3,64,64]{4,3,2,1,0:T(8,128)(2,1)}, u32[]{:S(2)}) copy-start(bf16[3,3,3,64,64]{4,3,2,1,0:T(8,128)(2,1)} %w_ref.1) | copy-start | bytes 663556
  1.6 0.9 %copy-start.1 = (bf16[1,1,16,4096]{3,2,1,0:T(8,128)(2,1)S(1)}, bf16[1,1,16,4096]{3,2,1,0:T(8,128)(2,1)}, u32[]{:S(2)}) copy-start(bf16[1,1,16,4096]{3,2,1,0:T(8,128)(2,1)} %x_ref.1) | copy-start | bytes 393220
  2.5 0.9 %copy-start.2 = (bf16[1,1,16,4096]{3,2,1,0:T(8,128)(2,1)S(1)}, bf16[1,1,16,4096]{3,2,1,0:T(8,128)(2,1)}, u32[]{:S(2)}) copy-start(bf16[1,1,16,4096]{3,2,1,0:T(8,128)(2,1)} %z_ref.1) | copy-start | bytes 393220
  3.5 0.9 %copy-start.3 = (bf16[1,1,16,4096]{3,2,1,0:T(8,128)(2,1)S(1)}, bf16[1,1,16,4096]{3,2,1,0:T(8,128)(2,1)}, u32[]{:S(2)}) copy-start(bf16[1,1,16,4096]{3,2,1,0:T(8,128)(2,1)} %dy_ref.1) | copy-start | bytes 393220
